TPU v7x, 32 devices: a whole 2x2x4 slice. The times are simulated.
32 devices in a mesh: groups: 2 (over y), ctx: 4 (over z), head: 2 (over x), sub: 2 (over core).
Axes of the slice: x: 2, y: 2, z: 4, core: 2. Of those that a mesh axis runs over, the one named last changes fastest.
Arguments:
- hidden_in: bfloat16 [1024, 5120], P(('groups', 'ctx'), 'sub'), parts along dimension 0, may hold values from -6 to 6
- w_qkv: bfloat16 [5120, 8, 896], P('sub', 'head', 'ctx'), may hold values from -0.078125 to 0.078125
- qkv_bias: bfloat16 [8, 896], P('head'), may hold values from -3 to 3
- w_out: bfloat16 [8, 640, 5120], P('head', 'ctx'), may hold values from -0.078125 to 0.078125
- prev_keys: bfloat16 [1024, 8, 128], P(('groups', 'ctx', 'sub'), 'head'), parts along dimension 0, may hold values from -60 to 60
- prev_values: bfloat16 [1024, 8, 128], P(('groups', 'ctx', 'sub'), 'head'), parts along dimension 0, may hold values from -6 to 6
- shard_blocks: int32 [8], P('groups'), parts along dimension 0, may hold values from 0 to 3, each once
Outputs:
- attn_out: bfloat16 [1024, 5120], P(('groups', 'ctx', 'sub'), 'head'), parts along dimension 0
There are 2 independent parts, one for each index of `groups`. A program takes and returns all parts, laid end to end along the dimension named above; an argument that names none is the same for every part. Nothing has to cross between parts.
Inputs may be any that keep to these rules, and one draw needn't show every extreme that they name: Index c of ctx holds the positions shard_blocks[c] * 128 to shard_blocks[c] * 128 + 127; every block occurs once.
All inputs are finite; a program needn't handle non-finite values.
Results may differ from a plain program's by a relative error of at most 0.015.
The roundings to bfloat16 on the way count: a program that leaves them out, or rounds other values in their place, can miss the bound.
Values may be sent and summed in bfloat16 or wider, within the bound.
A program may use at most 64 MiB of HBM per device.

v0:
```python
import math

import jax
import jax.numpy as jnp
from jax import lax
from jax.sharding import PartitionSpec as P

G = 5
HD = 128
NPREV = 2


rope_base = 10000000.0
neg_big = -1e30


def rotate(vectors, positions):
    half_width = vectors.shape[-1] // 2
    frequency = rope_base ** (
        -(jnp.arange(half_width, dtype=jnp.float32) * 2.0) / vectors.shape[-1]
    )
    angles = positions.astype(jnp.float32)[:, None] * frequency[None, :]
    extra = (1,) * (vectors.ndim - 2)
    cosine = jnp.cos(angles).reshape((angles.shape[0],) + extra + (half_width,))
    sine_part = jnp.sin(angles).reshape((angles.shape[0],) + extra + (half_width,))
    first = vectors[..., :half_width]
    second = vectors[..., half_width:]
    return jnp.concatenate(
        [first * cosine - second * sine_part, second * cosine + first * sine_part], axis=-1
    )


def lookup(small_table, wanted):
    entries = jnp.arange(small_table.shape[0], dtype=jnp.int32)
    return jnp.sum(jnp.where(wanted[..., None] == entries, small_table, 0), axis=-1)


def local(hidden_in, w_qkv, qkv_bias, w_out, prev_keys, prev_values, shard_blocks):
    n_ctx = lax.axis_size("ctx")
    n_sub = lax.axis_size("sub")
    n_head = lax.axis_size("head")
    tok_ctx = hidden_in.shape[0]
    tok_dev = tok_ctx // n_sub
    span_len = tok_ctx * n_ctx // 2
    kv_dev = w_qkv.shape[1]
    me_ctx = lax.axis_index("ctx")
    me_sub = lax.axis_index("sub")
    partial_value = jnp.einsum(
        "td,dhn->thn",
        hidden_in,
        lax.all_gather(w_qkv, "ctx", axis=2, tiled=True),
        preferred_element_type=jnp.float32,
    )
    joined = lax.psum_scatter(partial_value, "sub", scatter_dimension=0, tiled=True)
    joined = (joined + qkv_bias.astype(jnp.float32)[None]).reshape(tok_dev, kv_dev, G + 2, HD)
    owner_block = lookup(shard_blocks, me_ctx)
    positions = owner_block * tok_ctx + me_sub * tok_dev + jnp.arange(tok_dev, dtype=jnp.int32)
    span_q = NPREV + positions // span_len
    local_q = positions % span_len
    queries = joined[:, :, :G]

    def arrange(rotated):
        return jnp.transpose(rotated.astype(jnp.bfloat16), (1, 0, 2, 3)).reshape(
            kv_dev, tok_dev * G, HD
        )

    q_intra = arrange(rotate(queries, local_q))
    q_succ = arrange(rotate(queries, local_q + span_len))
    q_inter = arrange(rotate(queries, jnp.full((tok_dev,), 2 * span_len - 1, jnp.int32)))
    k_cur = rotate(joined[:, :, G], local_q).astype(jnp.bfloat16)
    v_cur = joined[:, :, G + 1].astype(jnp.bfloat16)
    old_rows = (me_ctx * n_sub + me_sub) * tok_dev + jnp.arange(tok_dev, dtype=jnp.int32)
    k_prev = rotate(prev_keys.astype(jnp.float32), old_rows % span_len).astype(jnp.bfloat16)
    row_span = jnp.repeat(span_q, G)
    row_local = jnp.repeat(local_q, G)
    own_span = span_q[0]
    score_scale = HD ** (-0.5)
    row_count = tok_dev * G
    start_state = (
        jnp.full((kv_dev, row_count), neg_big, jnp.float32),
        jnp.zeros((kv_dev, row_count), jnp.float32),
        jnp.zeros((kv_dev, row_count, HD), jnp.float32),
    )

    def scores_of(query_set, key_block):
        return (
            jnp.einsum("hrd,khd->hrk", query_set, key_block, preferred_element_type=jnp.float32)
            * score_scale
        )

    def update(running, scores, allowed, value_block):
        running_max, weight_sum, weighted = running
        block_max = jnp.max(jnp.where(allowed, scores, neg_big), axis=2)
        new_max = jnp.maximum(running_max, block_max)
        weights = jnp.where(allowed, jnp.exp(scores - new_max[..., None]), 0.0)
        rescale = jnp.exp(running_max - new_max)
        weight_sum = weight_sum * rescale + jnp.sum(weights, axis=2)
        weighted = weighted * rescale[..., None] + jnp.einsum(
            "hrk,khd->hrd",
            weights.astype(jnp.bfloat16),
            value_block,
            preferred_element_type=jnp.float32,
        )
        return (new_max, weight_sum, weighted)

    def current_block(running, key_block, value_block, key_index):
        shard_index = key_index // tok_dev
        key_pos = (
            lookup(shard_blocks, shard_index // n_sub) * tok_ctx
            + shard_index % n_sub * tok_dev
            + key_index % tok_dev
        )
        key_span = NPREV + key_pos // span_len
        key_local = key_pos % span_len
        same_span = key_span[None, :] == row_span[:, None]
        before = key_span[None, :] == row_span[:, None] - 1
        allowed = same_span & (key_local[None, :] <= row_local[:, None]) | before
        query_set = jnp.where(key_span[0] == own_span, q_intra, q_succ)
        return update(running, scores_of(query_set, key_block), allowed[None], value_block)

    def earlier_block(running, key_block, value_block, key_index):
        block_span = key_index[0] // span_len
        query_set = jnp.where(block_span == own_span - 1, q_succ, q_inter)
        scores = scores_of(query_set, key_block)
        return update(running, scores, jnp.ones(scores.shape, jnp.bool_), value_block)

    cur_keys = lax.all_gather(k_cur, ("ctx", "sub"), axis=0, tiled=True)
    cur_values = lax.all_gather(v_cur, ("ctx", "sub"), axis=0, tiled=True)
    old_keys = lax.all_gather(k_prev, ("ctx", "sub"), axis=0, tiled=True)
    old_values = lax.all_gather(prev_values, ("ctx", "sub"), axis=0, tiled=True)
    piece_rows = cur_keys.shape[0]
    block_rows = math.gcd(piece_rows, tok_dev)

    def turn(turn_index, state_in):
        offset = turn_index * block_rows
        key_index = offset + jnp.arange(block_rows, dtype=jnp.int32)

        def take(values):
            return lax.dynamic_slice_in_dim(values, offset, block_rows, 0)

        state_in = current_block(state_in, take(cur_keys), take(cur_values), key_index)
        return earlier_block(state_in, take(old_keys), take(old_values), key_index)

    running_max, weight_sum, weighted = lax.fori_loop(
        0, piece_rows // block_rows, turn, start_state
    )
    head_out = (weighted / weight_sum[..., None]).astype(jnp.bfloat16)
    head_out = jnp.transpose(head_out.reshape(kv_dev, tok_dev, G, HD), (1, 0, 2, 3)).reshape(
        tok_dev, kv_dev, G * HD
    )
    group_cols = w_out.shape[2] // (n_head * n_sub)
    split_cols = w_out.reshape(kv_dev, w_out.shape[1], n_head, n_sub, group_cols)
    own_cols = lax.dynamic_index_in_dim(split_cols, me_sub, 3, keepdims=False).reshape(
        kv_dev, w_out.shape[1], n_head * group_cols
    )
    pair_heads = lax.all_gather(head_out, "sub", axis=0, tiled=True)
    summed = jnp.einsum(
        "thn,hnd->td",
        pair_heads,
        lax.all_gather(own_cols, "ctx", axis=1, tiled=True),
        preferred_element_type=jnp.float32,
    )
    shares = lax.psum_scatter(summed.astype(jnp.bfloat16), "head", scatter_dimension=1, tiled=True)
    return lax.all_to_all(shares, "sub", split_axis=0, concat_axis=1, tiled=True)


def solution(mesh):
    return jax.shard_map(
        local,
        mesh=mesh,
        in_specs=(
            P(("groups", "ctx"), "sub"),
            P("sub", "head", "ctx"),
            P("head", None),
            P("head", "ctx", None),
            P(("groups", "ctx", "sub"), "head", None),
            P(("groups", "ctx", "sub"), "head", None),
            P("groups"),
        ),
        out_specs=P(("groups", "ctx", "sub"), "head"),
        check_vma=False,
    )
```

profile of v0, /device:TPU:28, one launch (start us, length us, event | category | flops | bytes accessed | tf_op | source)
XLA Modules:
  0.0 693.4 jit_solution(7797207133418223826)
XLA Ops:
  7.3 313.6 %all-gather.4.cloned.1.call-done = bf16[2560,4,896]{0,2,1:T(8,128)(2,1)} async-done(((bf16[2560,4,224]{0,2,1:T(8,128)(2,1)}), bf16[2560,4,896]{0,2,1:T(8,128)(2,1)}) %all-gather.4.cloned.1.call-update) | async-done | bytes 18350096 | tf_op jit(solution)/shard_map/all_gather | solution.py:51
  320.9 13.3 %fusion.36 = f32[128,4,896]{2,0,1:T(8,128)} fusion(bf16[2560,4,896]{0,2,1:T(8,128)(2,1)} %all-gather.4.cloned.1.call-done, bf16[128,2560]{1,0:T(8,128)(2,1)S(1)} %copy-done), kind=kOutput, calls=%fused_computation.72 | convolution fusion | flops 2348810240 | bytes 20840448 | tf_op jit(solution)/shard_map/td,dhn->thn/dot_general | solution.py:48
  334.5 15.2 %reshape.509 = bf16[4,160,2,2,1280]{4,3,2,1,0:T(2,128)(2,1)} reshape(bf16[4,160,5120]{2,1,0:T(8,128)(2,1)} %param.12) | data formatting | bytes 13107200 | tf_op jit(solution)/shard_map/reshape | solution.py:152
  349.7 55.3 %dynamic-slice_reduce_fusion = bf16[4,160,2,1280]{3,2,1,0:T(2,128)(2,1)} fusion(bf16[4,160,2,2,1280]{4,3,2,1,0:T(2,128)(2,1)} %reshape.509, s32[]{:T(128)S(6)} %select_n.317), kind=kLoop, calls=%fused_computation.63 | loop fusion | bytes 6553604 | tf_op jit(solution)/shard_map/jit(dynamic_index_in_dim)/dynamic_slice | solution.py:153
  405.0 8.2 %reshape.510 = bf16[4,160,2560]{2,1,0:T(8,128)(2,1)} reshape(bf16[4,160,2,1280]{3,2,1,0:T(2,128)(2,1)} %dynamic-slice_reduce_fusion) | data formatting | bytes 6553600 | tf_op jit(solution)/shard_map/reshape | solution.py:153
  415.4 16.3 %all_gather.23 = bf16[512,4,128]{2,0,1:T(8,128)(2,1)S(1)} all-gather(bf16[64,4,128]{2,0,1:T(8,128)(2,1)S(1)} %pad_maximum_fusion.1), channel_id=1, replica_groups=mesh['groups'=2,'ctx'=4,'head'=2,'sub'=2] {'ctx','sub'}, dimensions={0}, use_global_device_ids=true | all-gather | bytes 589824 | tf_op jit(solution)/shard_map/all_gather | solution.py:129
  431.8 25.5 %all_gather.25 = bf16[512,4,128]{2,0,1:T(8,128)(2,1)} all-gather(bf16[64,4,128]{2,0,1:T(8,128)(2,1)S(1)} %copy.42), channel_id=1, replica_groups=mesh['groups'=2,'ctx'=4,'head'=2,'sub'=2] {'ctx','sub'}, dimensions={0}, use_global_device_ids=true | all-gather | bytes 589824 | tf_op jit(solution)/shard_map/all_gather | solution.py:130
  457.3 1.3 broadcast_add_fusion.1
  459.2 23.4 %all_gather.22 = bf16[512,4,128]{2,0,1:T(8,128)(2,1)} all-gather(bf16[64,4,128]{2,0,1:T(8,128)(2,1)S(1)} %pad_maximum_fusion), channel_id=1, replica_groups=mesh['groups'=2,'ctx'=4,'head'=2,'sub'=2] {'ctx','sub'}, dimensions={0}, use_global_device_ids=true | all-gather | bytes 589824 | tf_op jit(solution)/shard_map/all_gather | solution.py:127
  482.6 25.5 %all-gather = bf16[512,4,1,128]{3,2,0,1:T(2,128)(2,1)S(1)} all-gather(bf16[64,4,1,128]{3,2,0,1:T(2,128)(2,1)S(1)} %slice.97), channel_id=2, replica_groups=mesh['groups'=2,'ctx'=4,'head'=2,'sub'=2] {'ctx','sub'}, dimensions={0}, use_global_device_ids=true | all-gather | bytes 589824 | tf_op jit(solution)/shard_map/all_gather | solution.py:128
  508.3 1.1 subtract_convert_fusion
  511.9 34.2 %while.21 = (s32[]{:T(128)}, f32[4,320]{1,0:T(4,128)S(1)}, f32[4,320]{1,0:T(4,128)S(1)}, f32[4,320,128]{2,1,0:T(8,128)S(1)}, s32[4]{0:T(128)S(1)}, /*index=5*/s3...) while((s32[]{:T(128)}, f32[4,320]{1,0:T(4,128)S(1)}, ...), condition=%wide.region_8.9_spmd.clone, body=%wide.region_2.8_spmd.clone.sunk | while | flops 86380112 | bytes 6466017 | solution.py:144
  512.9 1.1 select_reduce_fusion.5
  515.0 1.2 convolution_add_fusion.3
  517.2 1.1 select_reduce_fusion.5
  519.3 1.2 convolution_add_fusion.3
  521.4 1.1 select_reduce_fusion.5
  523.6 1.2 convolution_add_fusion.3
  525.7 1.1 select_reduce_fusion.5
  527.9 1.2 convolution_add_fusion.3
  532.2 1.2 convolution_add_fusion.3
  534.3 1.1 select_reduce_fusion.5
  536.4 1.2 convolution_add_fusion.3
  538.5 1.1 select_reduce_fusion.5
  540.7 1.2 convolution_add_fusion.3
  542.8 1.1 select_reduce_fusion.5
  545.0 1.2 convolution_add_fusion.3
  547.2 2.4 all_gather.26
  549.6 106.9 %all-gather.6.cloned.1.call-done = bf16[4,640,2560]{2,1,0:T(8,128)(2,1)} async-done(((bf16[4,160,2560]{2,1,0:T(8,128)(2,1)}), bf16[4,640,2560]{2,1,0:T(8,128)(2,1)}) %all-gather.6.cloned.1.call-update) | async-done | bytes 13107216 | tf_op jit(solution)/shard_map/all_gather | solution.py:160
  656.5 7.5 %fusion.35 = bf16[128,2560]{1,0:T(8,128)(2,1)} fusion(bf16[128,4,640]{2,0,1:T(8,128)(2,1)S(1)} %all_gather.26, bf16[4,640,2560]{2,1,0:T(8,128)(2,1)} %all-gather.6.cloned.1.call-done), kind=kOutput, calls=%fused_computation.65 | convolution fusion | flops 1678049280 | bytes 14417920 | tf_op jit(solution)/shard_map/thn,hnd->td/dot_general | solution.py:157
  664.1 17.1 %reduce-scatter.5.cloned.1.call-done = bf16[128,1280]{1,0:T(8,128)(2,1)} async-done(((bf16[128,2560]{1,0:T(8,128)(2,1)}), bf16[128,1280]{1,0:T(8,128)(2,1)}) %reduce-scatter.5.cloned.1.call-update) | async-done | bytes 327696 | tf_op jit(solution)/shard_map/reduce_scatter | solution.py:163
  681.1 5.0 all_to_all.19
  (193 shorter events, 22.1 us)
Async XLA Ops:
  6.5 314.4 %copy-start = (bf16[128,2560]{1,0:T(8,128)(2,1)S(1)}, bf16[128,2560]{1,0:T(8,128)(2,1)}, u32[]{:S(2)}) copy-start(bf16[128,2560]{1,0:T(8,128)(2,1)} %param.9) | copy-start | bytes 1966084
  6.5 314.4 %all-gather.4.cloned.1.call-start = ((), (), s32[]{:S(2)}) async-start(), calls=%async_computation.3 | async-start | bytes 22937600 | tf_op jit(solution)/shard_map/all_gather | solution.py:51
  7.3 450.1 %reduce-scatter.3.cloned.1.call-start = ((), (), s32[]{:S(2)}) async-start(), calls=%async_computation.4 | async-start | bytes 2752512 | tf_op jit(solution)/shard_map/reduce_scatter | solution.py:54
  334.3 322.3 %all-gather.6.cloned.1.call-start = ((), (), s32[]{:S(2)}) async-start(), calls=%async_computation.5 | async-start | bytes 16384000 | tf_op jit(solution)/shard_map/all_gather | solution.py:160
  405.0 8.3 %copy-start.5 = (s32[4]{0:T(128)S(1)}, s32[4]{0:T(128)}, u32[]{:S(2)}) copy-start(s32[4]{0:T(128)} %param.15) | copy-start | bytes 52
  405.0 9.7 %copy-start.4 = (bf16[4,896]{1,0:T(4,128)(2,1)S(1)}, bf16[4,896]{1,0:T(4,128)(2,1)}, u32[]{:S(2)}) copy-start(bf16[4,896]{1,0:T(4,128)(2,1)} %param.11) | copy-start | bytes 21508
  405.0 9.7 %copy-start.3 = (bf16[64,4,128]{2,1,0:T(4,128)(2,1)S(1)}, bf16[64,4,128]{2,1,0:T(4,128)(2,1)}, u32[]{:S(2)}) copy-start(bf16[64,4,128]{2,1,0:T(4,128)(2,1)} %param.14) | copy-start | bytes 196612
  405.0 9.7 %copy-start.2 = (bf16[64,4,128]{2,1,0:T(4,128)(2,1)S(1)}, bf16[64,4,128]{2,1,0:T(4,128)(2,1)}, u32[]{:S(2)}) copy-start(bf16[64,4,128]{2,1,0:T(4,128)(2,1)} %param.13) | copy-start | bytes 196612
  413.3 267.8 %reduce-scatter.5.cloned.1.call-start = ((), (), s32[]{:S(2)}) async-start(), calls=%async_computation.6 | async-start | bytes 983040 | tf_op jit(solution)/shard_map/reduce_scatter | solution.py:163
  547.2 139.7 %copy-start.1 = (bf16[128,2560]{1,0:T(8,128)(2,1)S(1)}, bf16[128,2560]{1,0:T(8,128)(2,1)}, u32[]{:S(2)}) copy-start(bf16[128,2560]{1,0:T(8,128)(2,1)} %param.9) | copy-start | bytes 1966084
Sparse Core Ops, SparseCore 0:
  8.9 311.9 all-gather.3
  334.4 10.6 reduce-scatter.2
  413.4 243.0 all-gather.5
  664.2 16.8 reduce-scatter.4
where the time goes:
time: 697 us; the launch traced here: 693 us
  waiting for transfers between devices  438 us (63%)
  blocking collectives  98.2 us (14%)
  local copies, waits for them, and re-layouts  85.7 us (12%)
  matrix products  45.5 us (7%)
  between operations  14.1 us (2%)
  other arithmetic  8.88 us (1%)
    all_gather x1, waiting for transfers between devices, local(): lax.all_gather(w_qkv, 'ctx', axis=2, tiled=True)  314 us
    all_gather x1, waiting for transfers between devices, local(): lax.all_gather(own_cols, 'ctx', axis=1, tiled=True)  107 us
    dynamic_slice x1, local copies, waits for them, and re-layouts, local(): lax.dynamic_index_in_dim(split_cols, me_sub, 3, keepdims=False)  55.3 us
    all_gather x1, blocking collectives, local(): cur_values = lax.all_gather(v_cur, ('ctx', 'sub'), axis=0, tiled=True)  25.5 us
    all_gather x1, blocking collectives, local(): old_values = lax.all_gather(prev_values, ('ctx', 'sub'), axis=0, tiled=True)  25.5 us
    all_gather x1, blocking collectives, local(): cur_keys = lax.all_gather(k_cur, ('ctx', 'sub'), axis=0, tiled=True)  23.4 us
    reduce_scatter x1, waiting for transfers between devices, local(): lax.psum_scatter(summed.astype(jnp.bfloat16), 'head', scatter_dimension=1...  17.1 us
    all_gather x1, blocking collectives, local(): old_keys = lax.all_gather(k_prev, ('ctx', 'sub'), axis=0, tiled=True)  16.3 us
  transfers between devices with their start and end apart: 4, of which 3 were waited for; matrix products, arithmetic and copies ran while one was open for 17% of the time, Pallas kernels for 0%

commit v1 on v0

--- a/solution.py
+++ b/solution.py
@@ -1,8 +1,12 @@
+import functools
 import math
 
 import jax
 import jax.numpy as jnp
+import numpy as np
 from jax import lax
+from jax.experimental import pallas as pl
+from jax.experimental.pallas import tpu as pltpu
 from jax.sharding import PartitionSpec as P
 
 G = 5
@@ -164,9 +168,468 @@
     return lax.all_to_all(shares, "sub", split_axis=0, concat_axis=1, tiled=True)
 
 
+MESH = pl.DeviceIdType.MESH
+LANE = 128
+OUT_CHUNKS = 4
+
+
+def round_up(value, step):
+    return (value + step - 1) // step * step
+
+
+def remote(src, dst, send_sem, recv_sem, **where):
+    return pltpu.make_async_remote_copy(
+        src_ref=src, dst_ref=dst, send_sem=send_sem, recv_sem=recv_sem,
+        device_id=where, device_id_type=MESH,
+    )
+
+
+def rope_rows(vectors, cosine, sine):
+    return vectors * cosine + pltpu.roll(vectors, HD // 2, 1) * sine
+
+
+def fused(
+    sb, x_ref, pv_ref, bias, rope_c, rope_s, w_hbm, wo_hbm, out_ref,
+    hid, wv, wo, part, prcv, jb, ar, kv, old, qf, ho, a2, xs, xr, ow, zs, zr,
+    w_sem, zsr_sem, zsl_sem, zrv_sem, hs_sem, hr_sem, ps_sem, pr_sem, as_sem, ar_sem,
+    os_sem, or_sem, ex_sem, bs_sem, br_sem, cs_sem, cr_sem, ds_sem, dr_sem,
+):
+    n = hid.shape[0]
+    tok = hid.shape[1]
+    half = tok // 2
+    span_len = tok * n // 2
+    piece = w_hbm.shape[1]
+    wide = wv.shape[1]
+    rows_out = wo_hbm.shape[1]
+    chunks, _, _, chunk = xs.shape
+    c = lax.axis_index("ctx")
+    hx = lax.axis_index("head")
+    s = lax.axis_index("sub")
+    oh = 1 - hx
+    other = 1 - s
+
+    def others(action):
+        for j in range(n):
+            pl.when(c != j)(functools.partial(action, j))
+
+    for h in range(n):
+        wv[h, piece:, :] = jnp.zeros((wide - piece, wv.shape[2]), jnp.bfloat16)
+    load_w = pltpu.make_async_copy(w_hbm, wv.at[:, pl.ds(0, piece), :], w_sem.at[0])
+    load_w.start()
+
+    barrier = pltpu.get_barrier_semaphore()
+
+    def greet(j):
+        pl.semaphore_signal(barrier, inc=1, device_id={"ctx": j}, device_id_type=MESH)
+
+    others(greet)
+    pl.semaphore_signal(barrier, inc=1, device_id={"head": oh}, device_id_type=MESH)
+    pl.semaphore_signal(barrier, inc=1, device_id={"sub": other}, device_id_type=MESH)
+    pl.semaphore_wait(barrier, n + 1)
+
+    mine = pl.ds(pl.multiple_of(hx * half, half), half)
+    theirs = pl.ds(pl.multiple_of(oh * half, half), half)
+
+    def to_right(src, blk):
+        return remote(src, hid.at[blk, mine], zsr_sem.at[blk], zrv_sem.at[blk], ctx=c + 1)
+
+    def to_left(src, blk):
+        return remote(src, hid.at[blk, mine], zsl_sem.at[blk], zrv_sem.at[blk], ctx=c - 1)
+
+    def over_x(blk, rows):
+        return remote(hid.at[blk, rows], hid.at[blk, rows], hs_sem.at[blk], hr_sem.at[blk], head=oh)
+
+    pl.when(c + 1 < n)(lambda: to_right(x_ref.at[mine], c).start())
+    pl.when(c > 0)(lambda: to_left(x_ref.at[mine], c).start())
+
+    def old_copy(j, src_ctx):
+        return remote(pv_ref.at[j], old.at[s, src_ctx], os_sem.at[j], or_sem.at[src_ctx], ctx=j)
+
+    others(lambda j: old_copy(j, c).start())
+    old[s, c] = pv_ref[c]
+
+    wo[...] = jnp.zeros(wo.shape, jnp.bfloat16)
+    row_off = pl.multiple_of((c * rows_out) % LANE, 16)
+    load_wo = pltpu.make_async_copy(wo_hbm, wo.at[:, pl.ds(row_off, rows_out), :], w_sem.at[1])
+    load_wo.start()
+    load_w.wait()
+
+    def part_copy(blk):
+        return remote(part.at[blk, other], prcv.at[blk], ps_sem.at[blk], pr_sem.at[blk], sub=other)
+
+    def piece_copy(blk, j, src_ctx):
+        return remote(
+            jb.at[blk, j], ar.at[src_ctx, blk], as_sem.at[blk, j], ar_sem.at[src_ctx, blk], ctx=j
+        )
+
+    def project(blk, rows):
+        for h in range(n):
+            product = lax.dot_general(
+                rows, wv[h], (((1,), (1,)), ((), ())), preferred_element_type=jnp.float32
+            )
+            part[blk, 0, h] = product[:half]
+            part[blk, 1, h] = product[half:]
+        part_copy(blk).start()
+
+    def finish(blk):
+        part_copy(blk).wait_recv()
+        for h in range(n):
+            joined = part[blk, s, h] + prcv[blk, h] + bias[h : h + 1, :]
+            jb[blk, h] = joined.astype(jnp.bfloat16)
+        ar[c, blk] = jb[blk, c]
+        others(lambda j: piece_copy(blk, j, c).start())
+
+    project(c, x_ref[...])
+    finish(c)
+
+    def arrive(distance, carry):
+        left = c - distance
+        right = c + distance
+
+        def from_left():
+            to_right(hid.at[left, mine], left).wait_recv()
+            pl.when(c + 1 < n)(lambda: to_right(hid.at[left, mine], left).start())
+            over_x(left, mine).start()
+
+        def from_right():
+            to_left(hid.at[right, mine], right).wait_recv()
+            pl.when(c > 0)(lambda: to_left(hid.at[right, mine], right).start())
+            over_x(right, mine).start()
+
+        def use(blk):
+            over_x(blk, theirs).wait_recv()
+            project(blk, hid[blk])
+
+        pl.when(left >= 0)(from_left)
+        pl.when(right < n)(from_right)
+        pl.when(left >= 0)(lambda: use(left))
+        pl.when(right < n)(lambda: use(right))
+        pl.when(left >= 0)(lambda: finish(left))
+        pl.when(right < n)(lambda: finish(right))
+        return carry
+
+    lax.fori_loop(1, n, arrive, 0)
+
+    def old_ready(j):
+        old_copy(j, j).wait_recv()
+
+    others(old_ready)
+    for j in range(n):
+        at = pl.ds(pl.multiple_of(((j * 2 + s) * half) % span_len, half), half)
+        raw = old[s, j, 0].astype(jnp.float32)
+        old[s, j, 0] = rope_rows(raw, rope_c[at, :], rope_s[at, :]).astype(jnp.bfloat16)
+    old_pair = remote(old.at[s], old.at[s], ex_sem.at[0], ex_sem.at[1], sub=other)
+    old_pair.start()
+
+    lane = lax.broadcasted_iota(jnp.int32, (half, LANE), 1)
+
+    def block_rows(table, in_span, first):
+        chosen = None
+        for v in range(n // 2):
+            rows = table[pl.ds(pl.multiple_of(first + v * tok + s * half, half), half), :]
+            chosen = rows if chosen is None else jnp.where(in_span == v, rows, chosen)
+        return chosen
+
+    def gather_head(blk, carry):
+        others(lambda j: piece_copy(blk, j, j).wait_recv())
+        got = [ar[j, blk].astype(jnp.float32) for j in range(n)]
+        columns = []
+        for b in range(G + 2):
+            total = None
+            for j in range(n):
+                shift = b * LANE - j * piece
+                if shift <= -LANE or shift >= piece:
+                    continue
+                moved = pltpu.roll(got[j], (-shift) % wide, 1)[:, :LANE]
+                inside = (lane + shift >= 0) & (lane + shift < piece)
+                moved = jnp.where(inside, moved, 0.0)
+                total = moved if total is None else total + moved
+            columns.append(total)
+        for g in range(G):
+            qf[blk, g] = columns[g]
+        in_span = sb[blk] % (n // 2)
+        cosine, sine = block_rows(rope_c, in_span, 0), block_rows(rope_s, in_span, 0)
+        kv[s, 0, blk] = rope_rows(columns[G], cosine, sine).astype(jnp.bfloat16)
+        kv[s, 1, blk] = columns[G + 1].astype(jnp.bfloat16)
+        return carry
+
+    lax.fori_loop(0, n, gather_head, 0)
+    kv_pair = remote(kv.at[s], kv.at[s], ex_sem.at[2], ex_sem.at[3], sub=other)
+    kv_pair.start()
+    remote(old.at[other], old.at[other], ex_sem.at[0], ex_sem.at[1], sub=other).wait_recv()
+    remote(kv.at[other], kv.at[other], ex_sem.at[2], ex_sem.at[3], sub=other).wait_recv()
+
+    row_count = half * G
+    scale = HD ** (-0.5)
+    count = 2 * n * half
+    key = lax.broadcasted_iota(jnp.int32, (1, count), 1)
+    key_block = (key % (n * half)) // half
+    key_pos = (key // (n * half)) * half + key % half
+    for j in range(n):
+        key_pos = key_pos + jnp.where(key_block == j, sb[j] * tok, 0)
+    key_span = NPREV + key_pos // span_len
+    key_local = key_pos % span_len
+    row_in = lax.broadcasted_iota(jnp.int32, (row_count, 1), 0) % half
+    last = 2 * span_len - 1
+
+    def scores_of(query, keys):
+        return lax.dot_general(
+            query, keys, (((1,), (1,)), ((), ())), preferred_element_type=jnp.float32
+        ) * scale
+
+    def head_copy(blk, j, src_ctx):
+        first = (j * rows_out) // LANE * LANE
+        return remote(
+            ho.at[blk, :, pl.ds(first, a2.shape[3])], a2.at[src_ctx, blk],
+            bs_sem.at[blk, j], br_sem.at[src_ctx, blk], ctx=j,
+        )
+
+    def attend(blk, carry):
+        first_pos = sb[blk] * tok
+        span = NPREV + first_pos // span_len
+        local_first = first_pos % span_len + s * half
+        in_span = sb[blk] % (n // 2)
+
+        def query_set(cosine, sine):
+            return jnp.concatenate(
+                [rope_rows(qf[blk, g], cosine, sine) for g in range(G)], axis=0
+            ).astype(jnp.bfloat16)
+
+        q_intra = query_set(block_rows(rope_c, in_span, 0), block_rows(rope_s, in_span, 0))
+        q_succ = query_set(
+            block_rows(rope_c, in_span, span_len), block_rows(rope_s, in_span, span_len)
+        )
+        q_inter = query_set(rope_c[last : last + 1, :], rope_s[last : last + 1, :])
+        keys = kv[:, 0].reshape(2, n * half, HD).reshape(count, HD)
+        values = kv[:, 1].reshape(2, n * half, HD).reshape(count, HD)
+        same = key_span == span
+        before = key_span == span - 1
+        score = jnp.where(same, scores_of(q_intra, keys), scores_of(q_succ, keys))
+        allowed = (same & (key_local <= row_in + local_first)) | before
+        score = jnp.where(allowed, score, neg_big)
+        pieces = [(score, values)]
+        per_span = n // NPREV
+        for b in range(NPREV):
+            block = old[:, b * per_span : (b + 1) * per_span]
+            size = 2 * per_span * half
+            s_succ = scores_of(q_succ, block[:, :, 0].reshape(size, HD))
+            s_inter = scores_of(q_inter, block[:, :, 0].reshape(size, HD))
+            pieces.append((jnp.where(span - 1 == b, s_succ, s_inter), block[:, :, 1].reshape(size, HD)))
+        top = functools.reduce(
+            jnp.maximum, [jnp.max(score, axis=1, keepdims=True) for score, _ in pieces]
+        )
+        weight_sum = jnp.zeros((row_count, 1), jnp.float32)
+        weighted = jnp.zeros((row_count, HD), jnp.float32)
+        for score, value in pieces:
+            weights = jnp.exp(score - top)
+            weight_sum = weight_sum + jnp.sum(weights, axis=1, keepdims=True)
+            weighted = weighted + jnp.dot(
+                weights.astype(jnp.bfloat16), value, preferred_element_type=jnp.float32
+            )
+        result = (weighted / weight_sum).astype(jnp.bfloat16)
+        for g in range(G):
+            ho[blk, :, g * HD : (g + 1) * HD] = result[g * half : (g + 1) * half]
+
+        def keep(j):
+            first = (j * rows_out) // LANE * LANE
+            a2[j, blk] = ho[blk, :, first : first + a2.shape[3]]
+
+        for j in range(n):
+            pl.when(c == j)(functools.partial(keep, j))
+        others(lambda j: head_copy(blk, j, c).start())
+        return carry
+
+    lax.fori_loop(0, n, attend, 0)
+    load_wo.wait()
+
+    def heads_ready(blk, carry):
+        others(lambda j: head_copy(blk, j, j).wait_recv())
+        return carry
+
+    lax.fori_loop(0, n, heads_ready, 0)
+
+    def product(column_first):
+        columns = pl.ds(pl.multiple_of(column_first, LANE), chunk)
+        total = None
+        for j in range(n):
+            term = jnp.dot(
+                a2[j].reshape(n * half, a2.shape[3]), wo[j, :, columns],
+                preferred_element_type=jnp.float32,
+            )
+            total = term if total is None else total + term
+        return total.reshape(n, half, chunk)
+
+    width = chunk * chunks
+
+    def x_copy(k):
+        return remote(xs.at[k], xr.at[k], cs_sem.at[k], cr_sem.at[k], head=oh)
+
+    def z_copy(k, j, src_ctx):
+        return remote(
+            zs.at[k, j], zr.at[src_ctx, k], ds_sem.at[k, j], dr_sem.at[src_ctx, k], ctx=j
+        )
+
+    def send_half(k, carry):
+        xs[k] = product(oh * width + k * chunk).astype(jnp.bfloat16)
+        x_copy(k).start()
+        return carry
+
+    def own_half(k, carry):
+        ow[k] = product(hx * width + k * chunk)
+        return carry
+
+    def add_half(k, carry):
+        x_copy(k).wait_recv()
+        zs[k] = (ow[k] + xr[k].astype(jnp.float32)).astype(jnp.bfloat16)
+        others(lambda j: z_copy(k, j, c).start())
+        zr[c, k] = zs[k, c]
+        return carry
+
+    lax.fori_loop(0, chunks, send_half, 0)
+    lax.fori_loop(0, chunks, own_half, 0)
+    lax.fori_loop(0, chunks, add_half, 0)
+
+    for k in range(chunks):
+        others(lambda j: z_copy(k, j, j).wait_recv())
+        total = zr[0, k].astype(jnp.float32)
+        for j in range(1, n):
+            total = total + zr[j, k].astype(jnp.float32)
+        out_ref[:, k * chunk : (k + 1) * chunk] = total.astype(jnp.bfloat16)
+
+    old_pair.wait_send()
+    kv_pair.wait_send()
+    others(lambda j: old_copy(j, c).wait_send())
+    part_copy(c).wait_send()
+    pl.when(c + 1 < n)(lambda: to_right(x_ref.at[mine], c).wait_send())
+    pl.when(c > 0)(lambda: to_left(x_ref.at[mine], c).wait_send())
+
+    def sent(distance, carry):
+        left = c - distance
+        right = c + distance
+
+        def left_sent():
+            pl.when(c + 1 < n)(lambda: to_right(hid.at[left, mine], left).wait_send())
+            over_x(left, mine).wait_send()
+            part_copy(left).wait_send()
+
+        def right_sent():
+            pl.when(c > 0)(lambda: to_left(hid.at[right, mine], right).wait_send())
+            over_x(right, mine).wait_send()
+            part_copy(right).wait_send()
+
+        pl.when(left >= 0)(left_sent)
+        pl.when(right < n)(right_sent)
+        return carry
+
+    lax.fori_loop(1, n, sent, 0)
+
+    def block_sent(blk, carry):
+        others(lambda j: piece_copy(blk, j, c).wait_send())
+        others(lambda j: head_copy(blk, j, c).wait_send())
+        return carry
+
+    lax.fori_loop(0, n, block_sent, 0)
+
+    def chunk_sent(k, carry):
+        x_copy(k).wait_send()
+        others(lambda j: z_copy(k, j, c).wait_send())
+        return carry
+
+    lax.fori_loop(0, chunks, chunk_sent, 0)
+
+
+def rope_tables(count):
+    frequency = np.float32(rope_base) ** (
+        -(np.arange(HD // 2, dtype=np.float32) * np.float32(2.0)) / np.float32(HD)
+    )
+    angles = np.arange(count, dtype=np.float32)[:, None] * frequency.astype(np.float32)[None, :]
+    cosine = np.cos(angles.astype(np.float64)).astype(np.float32)
+    sine = np.sin(angles.astype(np.float64)).astype(np.float32)
+    return (
+        np.concatenate([cosine, cosine], axis=1),
+        np.concatenate([-sine, sine], axis=1),
+    )
+
+
+def local_fused(hidden_in, w_qkv, qkv_bias, w_out, prev_keys, prev_values, shard_blocks):
+    n = lax.axis_size("ctx")
+    tok, features = hidden_in.shape
+    half = tok // 2
+    piece = w_qkv.shape[2]
+    wide = round_up(piece, LANE)
+    rows_out, model = w_out.shape[1:]
+    window = 2 * LANE
+    chunks = OUT_CHUNKS
+    chunk = model // 2 // chunks
+    c = lax.axis_index("ctx")
+    bias = lax.dynamic_slice_in_dim(qkv_bias, c * piece, piece, 1).astype(jnp.float32)
+    bias = jnp.pad(bias, ((0, 0), (0, wide - piece)))
+    earlier = jnp.transpose(jnp.stack([prev_keys, prev_values]), (2, 0, 1, 3))
+    cosine, sine = rope_tables(tok * n)
+    bf16, f32, dma = jnp.bfloat16, jnp.float32, pltpu.SemaphoreType.DMA
+    vmem = pl.BlockSpec(memory_space=pltpu.VMEM)
+    smem = pl.BlockSpec(memory_space=pltpu.SMEM)
+    hbm = pl.BlockSpec(memory_space=pl.ANY)
+    return pl.pallas_call(
+        fused,
+        out_shape=jax.ShapeDtypeStruct((half, model // 2), bf16),
+        in_specs=[smem, vmem, vmem, vmem, vmem, vmem, hbm, hbm],
+        out_specs=vmem,
+        scratch_shapes=[
+            pltpu.VMEM((n, tok, features), bf16),
+            pltpu.VMEM((n, wide, features), bf16),
+            pltpu.VMEM((n, window, model), bf16),
+            pltpu.VMEM((n, 2, n, half, wide), f32),
+            pltpu.VMEM((n, n, half, wide), f32),
+            pltpu.VMEM((n, n, half, wide), bf16),
+            pltpu.VMEM((n, n, half, wide), bf16),
+            pltpu.VMEM((2, 2, n, half, HD), bf16),
+            pltpu.VMEM((2, n, 2, half, HD), bf16),
+            pltpu.VMEM((n, G, half, HD), f32),
+            pltpu.VMEM((n, half, G * HD), bf16),
+            pltpu.VMEM((n, n, half, window), bf16),
+            pltpu.VMEM((chunks, n, half, chunk), bf16),
+            pltpu.VMEM((chunks, n, half, chunk), bf16),
+            pltpu.VMEM((chunks, n, half, chunk), f32),
+            pltpu.VMEM((chunks, n, half, chunk), bf16),
+            pltpu.VMEM((n, chunks, half, chunk), bf16),
+            dma((2,)), dma((n,)), dma((n,)), dma((n,)), dma((n,)), dma((n,)), dma((n,)), dma((n,)),
+            dma((n, n)), dma((n, n)), dma((n,)), dma((n,)), dma((4,)), dma((n, n)), dma((n, n)),
+            dma((chunks,)), dma((chunks,)), dma((chunks, n)), dma((n, chunks)),
+        ],
+        compiler_params=pltpu.CompilerParams(
+            collective_id=0, has_side_effects=True, vmem_limit_bytes=56 * 2**20
+        ),
+    )(
+        shard_blocks, hidden_in, earlier, bias, jnp.asarray(cosine), jnp.asarray(sine),
+        jnp.transpose(w_qkv, (1, 2, 0)), w_out,
+    )
+
+
+def choose(hidden_in, w_qkv, qkv_bias, w_out, prev_keys, prev_values, shard_blocks):
+    n = lax.axis_size("ctx")
+    tok = hidden_in.shape[0]
+    rows_out, model = w_out.shape[1:]
+    offsets = [(j * rows_out) % LANE for j in range(n)]
+    fits = (
+        lax.axis_size("sub") == 2
+        and lax.axis_size("head") == 2
+        and w_qkv.shape[1] == n
+        and n % NPREV == 0
+        and tok % 32 == 0
+        and w_qkv.shape[2] % 16 == 0
+        and rows_out % 16 == 0
+        and max(offsets) + rows_out <= 2 * LANE
+        and ((n - 1) * rows_out) // LANE * LANE + 2 * LANE <= G * HD
+        and model % (2 * OUT_CHUNKS * LANE) == 0
+    )
+    body = local_fused if fits else local
+    return body(hidden_in, w_qkv, qkv_bias, w_out, prev_keys, prev_values, shard_blocks)
+
+
 def solution(mesh):
     return jax.shard_map(
-        local,
+        choose,
         mesh=mesh,
         in_specs=(
             P(("groups", "ctx"), "sub"),

time: 697 us -> 120 us (0.17)
  waiting for transfers between devices: 438 us -> 0 us
  Pallas kernels: 0 us -> 115 us
  blocking collectives: 98.2 us -> 0 us
  local copies, waits for them, and re-layouts: 85.7 us -> 3.38 us
  matrix products: 45.5 us -> 0 us
  between operations: 14.1 us -> 0.01 us
  other arithmetic: 8.88 us -> 1.26 us
    all_gather x2 -> x0, waiting for transfers between devices: 421 us -> none  [the longest x1 314 us: local(): lax.all_gather(w_qkv, 'ctx', axis=2, tiled=True)]
    pallas_call x0 -> x1, Pallas kernels: none -> 115 us  [local_fused(): pl.pallas_call(fused, out_shape=jax.ShapeDtypeStruct((half, model // 2),...]
    all_gather x5 -> x0, blocking collectives: 93.2 us -> none  [the longest x1 25.5 us: local(): cur_values = lax.all_gather(v_cur, ('ctx', 'sub'), axis=0, tiled=True)]
    dynamic_slice x1, local copies, waits for them, and re-layouts: 55.3 us -> 0.08 us  [local_fused(): lax.dynamic_slice_in_dim(qkv_bias, c * piece, piece, 1).astype(jnp.float32)]
    dot_general x34 -> x0, matrix products: 45.5 us -> none  [the longest x16 13.8 us: update(): jnp.einsum('hrk,khd->hrd', weights.astype(jnp.bfloat16), value_block, pre...]
    reshape x4 -> x0, local copies, waits for them, and re-layouts: 24 us -> none  [the longest x1 15.2 us: local(): w_out.reshape(kv_dev, w_out.shape[1], n_head, n_sub, group_cols)]
    reduce_scatter x2 -> x0, waiting for transfers between devices: 17.1 us -> none  [the longest x1 17.1 us: local(): lax.psum_scatter(summed.astype(jnp.bfloat16), 'head', scatter_dimension=1...]
  transfers between devices with their start and end apart: 4 -> 0, of which waited for: 3 -> 0; matrix products, arithmetic and copies ran while one was open for 17% -> 0% of each run, Pallas kernels for 0% -> 0%
where the time goes in v1:
time: 120 us; the launch traced here: 119 us
  Pallas kernels  115 us (96%)
  local copies, waits for them, and re-layouts  3.38 us (3%)
  other arithmetic  1.26 us (1%)
    pallas_call x1, Pallas kernels, local_fused(): pl.pallas_call(fused, out_shape=jax.ShapeDtypeStruct((half, model // 2),...  115 us
    unnamed x3, local copies, waits for them, and re-layouts  2.41 us

profile of v1, /device:TPU:28, one launch (start us, length us, event | category | flops | bytes accessed | tf_op | source)
XLA Modules:
  0.0 119.4 jit_solution(195004532273800977)
XLA Ops:
  0.0 0.0 copy-start
  0.0 0.7 copy-done
  0.7 0.1 constant_dynamic-slice_fusion
  0.8 0.6 pad_convert_fusion.bias
  1.4 0.9 copy_bitcast_fusion
  2.3 0.7 maximum_bitcast_fusion.pv_ref
  2.9 114.8 %shard_map.91 = bf16[64,2560]{1,0:T(8,128)(2,1)} custom-call(s32[4]{0:T(128)} %sb.1, bf16[128,2560]{1,0:T(8,128)(2,1)} %x_ref.1, bf16[4,2,64,128]{3,2,1,0:T(8,128)(2,1)} %maximum_bitcast_fusion.pv_ref, f32[4,256]{1,0:T(4,128)} %pad_convert_fusion.bias, f32[512,128]{1,0:T(8,128)} %constant.18.clone.rope_c, f32[512,128]{1,0:T(8,128)} %constant.19.clone.rope_s, ...), custom_call_target="tpu_custom_call" | custom-call | tf_op jit(solution)/shard_map/pallas_call | solution.py:573
  117.7 1.7 %copy.15 = bf16[64,2560]{1,0:T(8,128)(2,1)} copy(bf16[64,2560]{1,0:T(8,128)(2,1)} %shard_map.91) | data formatting | bytes 655360
Async XLA Ops:
  0.0 0.7 copy-start

commit v2 on v1

--- a/solution.py
+++ b/solution.py
@@ -170,7 +170,8 @@
 
 MESH = pl.DeviceIdType.MESH
 LANE = 128
-OUT_CHUNKS = 4
+OUT_CHUNKS = 5
+ROW_PIECES = 2
 
 
 def round_up(value, step):
@@ -227,20 +228,32 @@
     pl.semaphore_signal(barrier, inc=1, device_id={"sub": other}, device_id_type=MESH)
     pl.semaphore_wait(barrier, n + 1)
 
-    mine = pl.ds(pl.multiple_of(hx * half, half), half)
-    theirs = pl.ds(pl.multiple_of(oh * half, half), half)
-
-    def to_right(src, blk):
-        return remote(src, hid.at[blk, mine], zsr_sem.at[blk], zrv_sem.at[blk], ctx=c + 1)
-
-    def to_left(src, blk):
-        return remote(src, hid.at[blk, mine], zsl_sem.at[blk], zrv_sem.at[blk], ctx=c - 1)
-
-    def over_x(blk, rows):
-        return remote(hid.at[blk, rows], hid.at[blk, rows], hs_sem.at[blk], hr_sem.at[blk], head=oh)
-
-    pl.when(c + 1 < n)(lambda: to_right(x_ref.at[mine], c).start())
-    pl.when(c > 0)(lambda: to_left(x_ref.at[mine], c).start())
+    sliver = half // ROW_PIECES
+
+    def rows_of(chip, p):
+        return pl.ds(pl.multiple_of(chip * half + p * sliver, sliver), sliver)
+
+    def to_right(src, blk, p):
+        rows = rows_of(hx, p)
+        return remote(
+            src.at[rows], hid.at[blk, rows], zsr_sem.at[blk, p], zrv_sem.at[blk, p], ctx=c + 1
+        )
+
+    def to_left(src, blk, p):
+        rows = rows_of(hx, p)
+        return remote(
+            src.at[rows], hid.at[blk, rows], zsl_sem.at[blk, p], zrv_sem.at[blk, p], ctx=c - 1
+        )
+
+    def over_x(blk, chip, p):
+        rows = rows_of(chip, p)
+        return remote(
+            hid.at[blk, rows], hid.at[blk, rows], hs_sem.at[blk, p], hr_sem.at[blk, p], head=oh
+        )
+
+    for p in range(ROW_PIECES):
+        pl.when(c + 1 < n)(lambda: to_right(x_ref, c, p).start())
+        pl.when(c > 0)(lambda: to_left(x_ref, c, p).start())
 
     def old_copy(j, src_ctx):
         return remote(pv_ref.at[j], old.at[s, src_ctx], os_sem.at[j], or_sem.at[src_ctx], ctx=j)
@@ -279,36 +292,52 @@
         ar[c, blk] = jb[blk, c]
         others(lambda j: piece_copy(blk, j, c).start())
 
-    project(c, x_ref[...])
-    finish(c)
-
-    def arrive(distance, carry):
+    def pass_on(distance, p):
         left = c - distance
         right = c + distance
 
         def from_left():
-            to_right(hid.at[left, mine], left).wait_recv()
-            pl.when(c + 1 < n)(lambda: to_right(hid.at[left, mine], left).start())
-            over_x(left, mine).start()
+            to_right(hid.at[left], left, p).wait_recv()
+            pl.when(c + 1 < n)(lambda: to_right(hid.at[left], left, p).start())
+            over_x(left, hx, p).start()
 
         def from_right():
-            to_left(hid.at[right, mine], right).wait_recv()
-            pl.when(c > 0)(lambda: to_left(hid.at[right, mine], right).start())
-            over_x(right, mine).start()
-
-        def use(blk):
-            over_x(blk, theirs).wait_recv()
-            project(blk, hid[blk])
+            to_left(hid.at[right], right, p).wait_recv()
+            pl.when(c > 0)(lambda: to_left(hid.at[right], right, p).start())
+            over_x(right, hx, p).start()
 
         pl.when(left >= 0)(from_left)
         pl.when(right < n)(from_right)
-        pl.when(left >= 0)(lambda: use(left))
-        pl.when(right < n)(lambda: use(right))
-        pl.when(left >= 0)(lambda: finish(left))
-        pl.when(right < n)(lambda: finish(right))
-        return carry
-
-    lax.fori_loop(1, n, arrive, 0)
+
+    def use(blk):
+        for p in range(ROW_PIECES):
+            over_x(blk, oh, p).wait_recv()
+        project(blk, hid[blk])
+
+    def both(distance, action, p=None):
+        left = c - distance
+        right = c + distance
+        if p != 1:
+            pl.when(left >= 0)(lambda: action(left))
+        if p != 0:
+            pl.when(right < n)(lambda: action(right))
+
+    def arrive(distance, carry):
+        pass_on(distance, 0)
+        both(distance - 1, use, 0)
+        pass_on(distance, 1)
+        both(distance - 1, use, 1)
+        pl.when(distance == 2)(lambda: finish(c))
+        pl.when(distance > 2)(lambda: both(distance - 2, finish))
+        return carry
+
+    pass_on(1, 0)
+    project(c, x_ref[...])
+    pass_on(1, 1)
+    lax.fori_loop(2, n, arrive, 0)
+    both(n - 2, finish)
+    both(n - 1, use)
+    both(n - 1, finish)
 
     def old_ready(j):
         old_copy(j, j).wait_recv()
@@ -360,22 +389,16 @@
     remote(kv.at[other], kv.at[other], ex_sem.at[2], ex_sem.at[3], sub=other).wait_recv()
 
     row_count = half * G
-    scale = HD ** (-0.5)
-    count = 2 * n * half
-    key = lax.broadcasted_iota(jnp.int32, (1, count), 1)
-    key_block = (key % (n * half)) // half
-    key_pos = (key // (n * half)) * half + key % half
-    for j in range(n):
-        key_pos = key_pos + jnp.where(key_block == j, sb[j] * tok, 0)
-    key_span = NPREV + key_pos // span_len
-    key_local = key_pos % span_len
-    row_in = lax.broadcasted_iota(jnp.int32, (row_count, 1), 0) % half
+    key = lax.broadcasted_iota(jnp.int32, (row_count, tok), 1)
+    row = lax.broadcasted_iota(jnp.int32, (row_count, tok), 0) % half
+    ahead = key - row
     last = 2 * span_len - 1
+    power = HD ** (-0.5) * math.log2(math.e)
 
     def scores_of(query, keys):
         return lax.dot_general(
             query, keys, (((1,), (1,)), ((), ())), preferred_element_type=jnp.float32
-        ) * scale
+        )
 
     def head_copy(blk, j, src_ctx):
         first = (j * rows_out) // LANE * LANE
@@ -400,28 +423,33 @@
             block_rows(rope_c, in_span, span_len), block_rows(rope_s, in_span, span_len)
         )
         q_inter = query_set(rope_c[last : last + 1, :], rope_s[last : last + 1, :])
-        keys = kv[:, 0].reshape(2, n * half, HD).reshape(count, HD)
-        values = kv[:, 1].reshape(2, n * half, HD).reshape(count, HD)
-        same = key_span == span
-        before = key_span == span - 1
-        score = jnp.where(same, scores_of(q_intra, keys), scores_of(q_succ, keys))
-        allowed = (same & (key_local <= row_in + local_first)) | before
-        score = jnp.where(allowed, score, neg_big)
-        pieces = [(score, values)]
+        pieces = []
+        for j in range(n):
+            key_first = sb[j] * tok
+            key_span = NPREV + key_first // span_len
+            same = key_span == span
+            reach = jnp.where(same, local_first - key_first % span_len, -2 * span_len)
+            reach = jnp.where(key_span == span - 1, 2 * span_len, reach)
+            query = jnp.where(same, q_intra, q_succ)
+            score = scores_of(query, kv[:, 0, j].reshape(tok, HD))
+            score = jnp.where(ahead <= reach, score, neg_big)
+            pieces.append((score, kv[:, 1, j].reshape(tok, HD)))
         per_span = n // NPREV
         for b in range(NPREV):
             block = old[:, b * per_span : (b + 1) * per_span]
             size = 2 * per_span * half
-            s_succ = scores_of(q_succ, block[:, :, 0].reshape(size, HD))
-            s_inter = scores_of(q_inter, block[:, :, 0].reshape(size, HD))
-            pieces.append((jnp.where(span - 1 == b, s_succ, s_inter), block[:, :, 1].reshape(size, HD)))
+            query = q_inter
+            if b == NPREV - 1:
+                query = jnp.where(span - 1 == b, q_succ, q_inter)
+            score = scores_of(query, block[:, :, 0].reshape(size, HD))
+            pieces.append((score, block[:, :, 1].reshape(size, HD)))
         top = functools.reduce(
             jnp.maximum, [jnp.max(score, axis=1, keepdims=True) for score, _ in pieces]
         )
         weight_sum = jnp.zeros((row_count, 1), jnp.float32)
         weighted = jnp.zeros((row_count, HD), jnp.float32)
         for score, value in pieces:
-            weights = jnp.exp(score - top)
+            weights = jnp.exp2((score - top) * power)
             weight_sum = weight_sum + jnp.sum(weights, axis=1, keepdims=True)
             weighted = weighted + jnp.dot(
                 weights.astype(jnp.bfloat16), value, preferred_element_type=jnp.float32
@@ -500,21 +528,24 @@
     kv_pair.wait_send()
     others(lambda j: old_copy(j, c).wait_send())
     part_copy(c).wait_send()
-    pl.when(c + 1 < n)(lambda: to_right(x_ref.at[mine], c).wait_send())
-    pl.when(c > 0)(lambda: to_left(x_ref.at[mine], c).wait_send())
+    for p in range(ROW_PIECES):
+        pl.when(c + 1 < n)(lambda: to_right(x_ref, c, p).wait_send())
+        pl.when(c > 0)(lambda: to_left(x_ref, c, p).wait_send())
 
     def sent(distance, carry):
         left = c - distance
         right = c + distance
 
         def left_sent():
-            pl.when(c + 1 < n)(lambda: to_right(hid.at[left, mine], left).wait_send())
-            over_x(left, mine).wait_send()
+            for p in range(ROW_PIECES):
+                pl.when(c + 1 < n)(lambda: to_right(hid.at[left], left, p).wait_send())
+                over_x(left, hx, p).wait_send()
             part_copy(left).wait_send()
 
         def right_sent():
-            pl.when(c > 0)(lambda: to_left(hid.at[right, mine], right).wait_send())
-            over_x(right, mine).wait_send()
+            for p in range(ROW_PIECES):
+                pl.when(c > 0)(lambda: to_left(hid.at[right], right, p).wait_send())
+                over_x(right, hx, p).wait_send()
             part_copy(right).wait_send()
 
         pl.when(left >= 0)(left_sent)
@@ -593,7 +624,7 @@
             pltpu.VMEM((chunks, n, half, chunk), f32),
             pltpu.VMEM((chunks, n, half, chunk), bf16),
             pltpu.VMEM((n, chunks, half, chunk), bf16),
-            dma((2,)), dma((n,)), dma((n,)), dma((n,)), dma((n,)), dma((n,)), dma((n,)), dma((n,)),
+            dma((2,)), *[dma((n, ROW_PIECES))] * 5, dma((n,)), dma((n,)),
             dma((n, n)), dma((n, n)), dma((n,)), dma((n,)), dma((4,)), dma((n, n)), dma((n, n)),
             dma((chunks,)), dma((chunks,)), dma((chunks, n)), dma((n, chunks)),
         ],
@@ -616,7 +647,8 @@
         and lax.axis_size("head") == 2
         and w_qkv.shape[1] == n
         and n % NPREV == 0
-        and tok % 32 == 0
+        and n > 2
+        and tok % (32 * ROW_PIECES) == 0
         and w_qkv.shape[2] % 16 == 0
         and rows_out % 16 == 0
         and max(offsets) + rows_out <= 2 * LANE

time: 120 us -> 102 us (0.85)
  the two profiles are of different devices: /device:TPU:28 before, /device:TPU:0 now
where the time goes in v2:
time: 102 us
  Pallas kernels  96.9 us (95%)
  local copies, waits for them, and re-layouts  3.38 us (3%)
  other arithmetic  1.26 us (1%)
    pallas_call x1, Pallas kernels, local_fused(): pl.pallas_call(fused, out_shape=jax.ShapeDtypeStruct((half, model // 2),...  96.9 us
    unnamed x3, local copies, waits for them, and re-layouts  2.41 us

profile of v2, /device:TPU:0, one launch (start us, length us, event | category | flops | bytes accessed | tf_op | source)
XLA Modules:
  0.0 101.6 jit_solution(12239648005476180465)
XLA Ops:
  0.0 0.0 copy-start
  0.0 0.7 copy-done
  0.7 0.1 constant_dynamic-slice_fusion
  0.8 0.6 pad_convert_fusion.bias
  1.4 0.9 copy_bitcast_fusion
  2.3 0.7 maximum_bitcast_fusion.pv_ref
  2.9 96.9 %shard_map.91 = bf16[64,2560]{1,0:T(8,128)(2,1)} custom-call(s32[4]{0:T(128)} %sb.1, bf16[128,2560]{1,0:T(8,128)(2,1)} %x_ref.1, bf16[4,2,64,128]{3,2,1,0:T(8,128)(2,1)} %maximum_bitcast_fusion.pv_ref, f32[4,256]{1,0:T(4,128)} %pad_convert_fusion.bias, f32[512,128]{1,0:T(8,128)} %constant.18.clone.rope_c, f32[512,128]{1,0:T(8,128)} %constant.19.clone.rope_s, ...), custom_call_target="tpu_custom_call" | custom-call | tf_op jit(solution)/shard_map/pallas_call | solution.py:604
  99.9 1.7 %copy.15 = bf16[64,2560]{1,0:T(8,128)(2,1)} copy(bf16[64,2560]{1,0:T(8,128)(2,1)} %shard_map.91) | data formatting | bytes 655360
Async XLA Ops:
  0.0 0.7 copy-start

commit v3 on v2

--- a/solution.py
+++ b/solution.py
@@ -202,7 +202,9 @@
     piece = w_hbm.shape[1]
     wide = wv.shape[1]
     rows_out = wo_hbm.shape[1]
-    chunks, _, _, chunk = xs.shape
+    per_half = xs.shape[1]
+    chunk = xs.shape[3]
+    chunks = zr.shape[1]
     c = lax.axis_index("ctx")
     hx = lax.axis_index("head")
     s = lax.axis_index("sub")
@@ -407,7 +409,8 @@
             bs_sem.at[blk, j], br_sem.at[src_ctx, blk], ctx=j,
         )
 
-    def attend(blk, carry):
+    def attend(turn, carry):
+        blk = (2 * turn) % n + (2 * turn) // n
         first_pos = sb[blk] * tok
         span = NPREV + first_pos // span_len
         local_first = first_pos % span_len + s * half
@@ -456,69 +459,94 @@
             )
         result = (weighted / weight_sum).astype(jnp.bfloat16)
         for g in range(G):
-            ho[blk, :, g * HD : (g + 1) * HD] = result[g * half : (g + 1) * half]
+            ho[turn, :, g * HD : (g + 1) * HD] = result[g * half : (g + 1) * half]
 
         def keep(j):
             first = (j * rows_out) // LANE * LANE
-            a2[j, blk] = ho[blk, :, first : first + a2.shape[3]]
+            a2[j, turn] = ho[turn, :, first : first + a2.shape[3]]
 
         for j in range(n):
             pl.when(c == j)(functools.partial(keep, j))
-        others(lambda j: head_copy(blk, j, c).start())
+        others(lambda j: head_copy(turn, j, c).start())
         return carry
 
-    lax.fori_loop(0, n, attend, 0)
-    load_wo.wait()
-
-    def heads_ready(blk, carry):
-        others(lambda j: head_copy(blk, j, j).wait_recv())
+    def heads_ready(turn, carry):
+        others(lambda j: head_copy(turn, j, j).wait_recv())
         return carry
 
-    lax.fori_loop(0, n, heads_ready, 0)
-
-    def product(column_first):
+    def product(part_index, column_first):
         columns = pl.ds(pl.multiple_of(column_first, LANE), chunk)
         total = None
         for j in range(n):
+            rows = a2[j, part_index * per_half : (part_index + 1) * per_half]
             term = jnp.dot(
-                a2[j].reshape(n * half, a2.shape[3]), wo[j, :, columns],
+                rows.reshape(per_half * half, a2.shape[3]), wo[j, :, columns],
                 preferred_element_type=jnp.float32,
             )
             total = term if total is None else total + term
-        return total.reshape(n, half, chunk)
+        return total.reshape(per_half, half, chunk)
 
     width = chunk * chunks
 
-    def x_copy(k):
-        return remote(xs.at[k], xr.at[k], cs_sem.at[k], cr_sem.at[k], head=oh)
-
-    def z_copy(k, j, src_ctx):
+    def x_copy(m):
+        return remote(xs.at[m], xr.at[m], cs_sem.at[m], cr_sem.at[m], head=oh)
+
+    def z_copy(q, k, i, src_ctx):
         return remote(
-            zs.at[k, j], zr.at[src_ctx, k], ds_sem.at[k, j], dr_sem.at[src_ctx, k], ctx=j
-        )
-
-    def send_half(k, carry):
-        xs[k] = product(oh * width + k * chunk).astype(jnp.bfloat16)
-        x_copy(k).start()
-        return carry
-
-    def own_half(k, carry):
-        ow[k] = product(hx * width + k * chunk)
-        return carry
-
-    def add_half(k, carry):
-        x_copy(k).wait_recv()
-        zs[k] = (ow[k] + xr[k].astype(jnp.float32)).astype(jnp.bfloat16)
-        others(lambda j: z_copy(k, j, c).start())
-        zr[c, k] = zs[k, c]
-        return carry
-
-    lax.fori_loop(0, chunks, send_half, 0)
-    lax.fori_loop(0, chunks, own_half, 0)
-    lax.fori_loop(0, chunks, add_half, 0)
+            zs.at[q * chunks + k, i], zr.at[src_ctx, k],
+            ds_sem.at[q * chunks + k, i], dr_sem.at[src_ctx, k], ctx=2 * i + q,
+        )
+
+    def send_half(q):
+        def send(k, carry):
+            m = q * chunks + k
+            xs[m] = product(q, oh * width + k * chunk).astype(jnp.bfloat16)
+            x_copy(m).start()
+            return carry
+
+        lax.fori_loop(0, chunks, send, 0)
+
+    def own_half(q):
+        def compute(k, carry):
+            ow[q * chunks + k] = product(q, hx * width + k * chunk)
+            return carry
+
+        lax.fori_loop(0, chunks, compute, 0)
+
+    def to_owners(q, action):
+        for i in range(per_half):
+            pl.when(c != 2 * i + q)(functools.partial(action, i))
+
+    def add_half(q):
+        def add(k, carry):
+            m = q * chunks + k
+            x_copy(m).wait_recv()
+            zs[m] = (ow[m] + xr[m].astype(jnp.float32)).astype(jnp.bfloat16)
+            to_owners(q, lambda i: z_copy(q, k, i, c).start())
+
+            def keep(i):
+                zr[2 * i + q, k] = zs[m, i]
+
+            for i in range(per_half):
+                pl.when(c == 2 * i + q)(functools.partial(keep, i))
+            return carry
+
+        lax.fori_loop(0, chunks, add, 0)
+
+    lax.fori_loop(0, n - 1, attend, 0)
+    load_wo.wait()
+    lax.fori_loop(0, per_half, heads_ready, 0)
+    send_half(0)
+    lax.fori_loop(n - 1, n, attend, 0)
+    own_half(0)
+    lax.fori_loop(per_half, n, heads_ready, 0)
+    send_half(1)
+    add_half(0)
+    own_half(1)
+    add_half(1)
 
     for k in range(chunks):
-        others(lambda j: z_copy(k, j, j).wait_recv())
+        others(lambda j: z_copy(0, k, 0, j).wait_recv())
         total = zr[0, k].astype(jnp.float32)
         for j in range(1, n):
             total = total + zr[j, k].astype(jnp.float32)
@@ -561,12 +589,13 @@
 
     lax.fori_loop(0, n, block_sent, 0)
 
-    def chunk_sent(k, carry):
-        x_copy(k).wait_send()
-        others(lambda j: z_copy(k, j, c).wait_send())
-        return carry
-
-    lax.fori_loop(0, chunks, chunk_sent, 0)
+    for q in range(2):
+        def chunk_sent(k, carry):
+            x_copy(q * chunks + k).wait_send()
+            to_owners(q, lambda i: z_copy(q, k, i, c).wait_send())
+            return carry
+
+        lax.fori_loop(0, chunks, chunk_sent, 0)
 
 
 def rope_tables(count):
@@ -619,14 +648,14 @@
             pltpu.VMEM((n, G, half, HD), f32),
             pltpu.VMEM((n, half, G * HD), bf16),
             pltpu.VMEM((n, n, half, window), bf16),
-            pltpu.VMEM((chunks, n, half, chunk), bf16),
-            pltpu.VMEM((chunks, n, half, chunk), bf16),
-            pltpu.VMEM((chunks, n, half, chunk), f32),
-            pltpu.VMEM((chunks, n, half, chunk), bf16),
+            pltpu.VMEM((2 * chunks, n // 2, half, chunk), bf16),
+            pltpu.VMEM((2 * chunks, n // 2, half, chunk), bf16),
+            pltpu.VMEM((2 * chunks, n // 2, half, chunk), f32),
+            pltpu.VMEM((2 * chunks, n // 2, half, chunk), bf16),
             pltpu.VMEM((n, chunks, half, chunk), bf16),
             dma((2,)), *[dma((n, ROW_PIECES))] * 5, dma((n,)), dma((n,)),
             dma((n, n)), dma((n, n)), dma((n,)), dma((n,)), dma((4,)), dma((n, n)), dma((n, n)),
-            dma((chunks,)), dma((chunks,)), dma((chunks, n)), dma((n, chunks)),
+            dma((2 * chunks,)), dma((2 * chunks,)), dma((2 * chunks, n // 2)), dma((n, chunks)),
         ],
         compiler_params=pltpu.CompilerParams(
             collective_id=0, has_side_effects=True, vmem_limit_bytes=56 * 2**20

time: 102 us -> 98.2 us (0.963)
  the two profiles are of different devices: /device:TPU:0 before, /device:TPU:28 now
where the time goes in v3:
time: 98.2 us; the launch traced here: 97.9 us
  Pallas kernels  93.3 us (95%)
  local copies, waits for them, and re-layouts  3.38 us (3%)
  other arithmetic  1.26 us (1%)
    pallas_call x1, Pallas kernels, local_fused(): pl.pallas_call(fused, out_shape=jax.ShapeDtypeStruct((half, model // 2),...  93.3 us
    unnamed x3, local copies, waits for them, and re-layouts  2.41 us

profile of v3, /device:TPU:28, one launch (start us, length us, event | category | flops | bytes accessed | tf_op | source)
XLA Modules:
  0.0 97.9 jit_solution(8643463446705786843)
XLA Ops:
  0.0 0.0 copy-start
  0.0 0.7 copy-done
  0.7 0.1 constant_dynamic-slice_fusion
  0.8 0.6 pad_convert_fusion.bias
  1.4 0.9 copy_bitcast_fusion
  2.3 0.7 maximum_bitcast_fusion.pv_ref
  2.9 93.3 %shard_map.91 = bf16[64,2560]{1,0:T(8,128)(2,1)} custom-call(s32[4]{0:T(128)} %sb.1, bf16[128,2560]{1,0:T(8,128)(2,1)} %x_ref.1, bf16[4,2,64,128]{3,2,1,0:T(8,128)(2,1)} %maximum_bitcast_fusion.pv_ref, f32[4,256]{1,0:T(4,128)} %pad_convert_fusion.bias, f32[512,128]{1,0:T(8,128)} %constant.18.clone.rope_c, f32[512,128]{1,0:T(8,128)} %constant.19.clone.rope_s, ...), custom_call_target="tpu_custom_call" | custom-call | tf_op jit(solution)/shard_map/pallas_call | solution.py:633
  96.2 1.7 %copy.15 = bf16[64,2560]{1,0:T(8,128)(2,1)} copy(bf16[64,2560]{1,0:T(8,128)(2,1)} %shard_map.91) | data formatting | bytes 655360
Async XLA Ops:
  0.0 0.7 copy-start

commit v4 on v3

--- a/solution.py
+++ b/solution.py
@@ -191,7 +191,7 @@
 
 def fused(
     sb, x_ref, pv_ref, bias, rope_c, rope_s, w_hbm, wo_hbm, out_ref,
-    hid, wv, wo, part, prcv, jb, ar, kv, old, qf, ho, a2, xs, xr, ow, zs, zr,
+    hid, wv, wo, part, prcv, jb, ar, kv, old, qf, ho, a2, a2r, xs, xr, ow, zs, zr,
     w_sem, zsr_sem, zsl_sem, zrv_sem, hs_sem, hr_sem, ps_sem, pr_sem, as_sem, ar_sem,
     os_sem, or_sem, ex_sem, bs_sem, br_sem, cs_sem, cr_sem, ds_sem, dr_sem,
 ):
@@ -264,9 +264,18 @@
     old[s, c] = pv_ref[c]
 
     wo[...] = jnp.zeros(wo.shape, jnp.bfloat16)
-    row_off = pl.multiple_of((c * rows_out) % LANE, 16)
-    load_wo = pltpu.make_async_copy(wo_hbm, wo.at[:, pl.ds(row_off, rows_out), :], w_sem.at[1])
-    load_wo.start()
+    rest = rows_out - LANE
+    groups = LANE // rest
+
+    def load_rows(u):
+        target = LANE if u == groups else pl.multiple_of(((u + c) % groups) * rest, rest)
+        return pltpu.make_async_copy(
+            wo_hbm.at[:, pl.ds(u * rest, rest), :], wo.at[:, pl.ds(target, rest), :],
+            w_sem.at[1 + u],
+        )
+
+    for u in range(groups + 1):
+        load_rows(u).start()
     load_w.wait()
 
     def part_copy(blk):
@@ -403,9 +412,8 @@
         )
 
     def head_copy(blk, j, src_ctx):
-        first = (j * rows_out) // LANE * LANE
         return remote(
-            ho.at[blk, :, pl.ds(first, a2.shape[3])], a2.at[src_ctx, blk],
+            ho.at[blk, j], a2r.at[src_ctx, blk],
             bs_sem.at[blk, j], br_sem.at[src_ctx, blk], ctx=j,
         )
 
@@ -457,21 +465,36 @@
             weighted = weighted + jnp.dot(
                 weights.astype(jnp.bfloat16), value, preferred_element_type=jnp.float32
             )
-        result = (weighted / weight_sum).astype(jnp.bfloat16)
-        for g in range(G):
-            ho[turn, :, g * HD : (g + 1) * HD] = result[g * half : (g + 1) * half]
-
-        def keep(j):
-            first = (j * rows_out) // LANE * LANE
-            a2[j, turn] = ho[turn, :, first : first + a2.shape[3]]
-
+        result = (weighted / weight_sum).astype(jnp.bfloat16).astype(jnp.float32)
+        few = half // groups
+        few_lane = lane[:few]
         for j in range(n):
-            pl.when(c == j)(functools.partial(keep, j))
+            first = result[j * half : (j + 1) * half]
+            second = result[(j + 1) * half : (j + 2) * half]
+            full = jnp.where(lane >= j * rest, first, second)
+            packed = jnp.zeros((few, LANE), jnp.float32)
+            for u in range(groups):
+                rows = second[u * few : (u + 1) * few]
+                shift = ((u - j) * rest) % LANE
+                moved = pltpu.roll(rows, shift, 1) if shift else rows
+                inside = (few_lane >= u * rest) & (few_lane < (u + 1) * rest)
+                packed = packed + jnp.where(inside, moved, 0.0)
+            ho[turn, j, :half, :] = full.astype(jnp.bfloat16)
+            ho[turn, j, half:, :] = packed.astype(jnp.bfloat16)
+
+        a2r[c, turn] = ho[turn, c]
         others(lambda j: head_copy(turn, j, c).start())
         return carry
 
     def heads_ready(turn, carry):
         others(lambda j: head_copy(turn, j, j).wait_recv())
+        few = half // groups
+        for j in range(n):
+            a2[j, turn, :, :LANE] = a2r[j, turn, :half, :]
+            packed = a2r[j, turn, half:, :].astype(jnp.float32)
+            for u in range(groups):
+                moved = pltpu.roll(packed, (LANE - u * rest) % LANE, 1) if u else packed
+                a2[j, turn, u * few : (u + 1) * few, LANE:] = moved.astype(jnp.bfloat16)
         return carry
 
     def product(part_index, column_first):
@@ -534,7 +557,8 @@
         lax.fori_loop(0, chunks, add, 0)
 
     lax.fori_loop(0, n - 1, attend, 0)
-    load_wo.wait()
+    for u in range(groups + 1):
+        load_rows(u).wait()
     lax.fori_loop(0, per_half, heads_ready, 0)
     send_half(0)
     lax.fori_loop(n - 1, n, attend, 0)
@@ -619,6 +643,8 @@
     wide = round_up(piece, LANE)
     rows_out, model = w_out.shape[1:]
     window = 2 * LANE
+    groups = LANE // (rows_out - LANE)
+    send_rows = half + half // groups
     chunks = OUT_CHUNKS
     chunk = model // 2 // chunks
     c = lax.axis_index("ctx")
@@ -646,14 +672,15 @@
             pltpu.VMEM((2, 2, n, half, HD), bf16),
             pltpu.VMEM((2, n, 2, half, HD), bf16),
             pltpu.VMEM((n, G, half, HD), f32),
-            pltpu.VMEM((n, half, G * HD), bf16),
+            pltpu.VMEM((n, n, send_rows, LANE), bf16),
             pltpu.VMEM((n, n, half, window), bf16),
+            pltpu.VMEM((n, n, send_rows, LANE), bf16),
             pltpu.VMEM((2 * chunks, n // 2, half, chunk), bf16),
             pltpu.VMEM((2 * chunks, n // 2, half, chunk), bf16),
             pltpu.VMEM((2 * chunks, n // 2, half, chunk), f32),
             pltpu.VMEM((2 * chunks, n // 2, half, chunk), bf16),
             pltpu.VMEM((n, chunks, half, chunk), bf16),
-            dma((2,)), *[dma((n, ROW_PIECES))] * 5, dma((n,)), dma((n,)),
+            dma((groups + 2,)), *[dma((n, ROW_PIECES))] * 5, dma((n,)), dma((n,)),
             dma((n, n)), dma((n, n)), dma((n,)), dma((n,)), dma((4,)), dma((n, n)), dma((n, n)),
             dma((2 * chunks,)), dma((2 * chunks,)), dma((2 * chunks, n // 2)), dma((n, chunks)),
         ],
@@ -670,7 +697,7 @@
     n = lax.axis_size("ctx")
     tok = hidden_in.shape[0]
     rows_out, model = w_out.shape[1:]
-    offsets = [(j * rows_out) % LANE for j in range(n)]
+    rest = rows_out - LANE
     fits = (
         lax.axis_size("sub") == 2
         and lax.axis_size("head") == 2
@@ -680,8 +707,11 @@
         and tok % (32 * ROW_PIECES) == 0
         and w_qkv.shape[2] % 16 == 0
         and rows_out % 16 == 0
-        and max(offsets) + rows_out <= 2 * LANE
-        and ((n - 1) * rows_out) // LANE * LANE + 2 * LANE <= G * HD
+        and rest > 0
+        and LANE == HD
+        and n * rest == LANE
+        and n + 1 == G
+        and tok // 2 * rest % (16 * LANE) == 0
         and model % (2 * OUT_CHUNKS * LANE) == 0
     )
     body = local_fused if fits else local

time: 98.2 us -> 97.2 us (0.990)
  Pallas kernels: 93.3 us -> 92.3 us
    pallas_call x1, Pallas kernels: 93.3 us -> 92.3 us  [local_fused(): pl.pallas_call(fused, out_shape=jax.ShapeDtypeStruct((half, model // 2),...]
where the time goes in v4:
time: 97.2 us; the launch traced here: 96.9 us
  Pallas kernels  92.3 us (95%)
  local copies, waits for them, and re-layouts  3.38 us (3%)
  other arithmetic  1.26 us (1%)
    pallas_call x1, Pallas kernels, local_fused(): pl.pallas_call(fused, out_shape=jax.ShapeDtypeStruct((half, model // 2),...  92.3 us
    unnamed x3, local copies, waits for them, and re-layouts  2.41 us

profile of v4, /device:TPU:28, one launch (start us, length us, event | category | flops | bytes accessed | tf_op | source)
XLA Modules:
  0.0 96.9 jit_solution(14828175563287389746)
XLA Ops:
  0.0 0.0 copy-start
  0.0 0.7 copy-done
  0.7 0.1 constant_dynamic-slice_fusion
  0.8 0.6 pad_convert_fusion.bias
  1.4 0.9 copy_bitcast_fusion
  2.3 0.7 maximum_bitcast_fusion.pv_ref
  2.9 92.3 %shard_map.91 = bf16[64,2560]{1,0:T(8,128)(2,1)} custom-call(s32[4]{0:T(128)} %sb.1, bf16[128,2560]{1,0:T(8,128)(2,1)} %x_ref.1, bf16[4,2,64,128]{3,2,1,0:T(8,128)(2,1)} %maximum_bitcast_fusion.pv_ref, f32[4,256]{1,0:T(4,128)} %pad_convert_fusion.bias, f32[512,128]{1,0:T(8,128)} %constant.18.clone.rope_c, f32[512,128]{1,0:T(8,128)} %constant.19.clone.rope_s, ...), custom_call_target="tpu_custom_call" | custom-call | tf_op jit(solution)/shard_map/pallas_call | solution.py:659
  95.2 1.7 %copy.15 = bf16[64,2560]{1,0:T(8,128)(2,1)} copy(bf16[64,2560]{1,0:T(8,128)(2,1)} %shard_map.91) | data formatting | bytes 655360
Async XLA Ops:
  0.0 0.7 copy-start
